TPU v7x, 32 devices: a whole 2x2x4 slice. The times are simulated.
32 devices in a mesh: dp: 8 (over z, x), tensor: 4 (over y, core).
Axes of the slice: x: 2, y: 2, z: 4, core: 2. Of those that a mesh axis runs over, the one named last changes fastest.
Arguments:
- images: bfloat16 [24, 729, 1152], P('dp', None, 'tensor'), may hold values from -6 to 6
- image_count: int32 [8], P('dp'), may hold values from 2 to 3, as said below
- attn_gain: float32 [1152], replicated, may hold values from 0.5 to 1.5
- attn_shift: float32 [1152], replicated, may hold values from -1.8 to 1.8
- query_weight: bfloat16 [1152, 1152], P('dp', 'tensor'), may hold values from -0.25 to 0.25
- query_bias: float32 [1152], P('tensor'), may hold values from -3 to 3
- key_weight: bfloat16 [1152, 1152], P('dp', 'tensor'), may hold values from -0.25 to 0.25
- value_weight: bfloat16 [1152, 1152], P('dp', 'tensor'), may hold values from -0.1875 to 0.1875
- value_bias: float32 [1152], P('tensor'), may hold values from -3 to 3
- output_weight: bfloat16 [1152, 1152], P('tensor', 'dp'), may hold values from -1 to 1
- output_bias: float32 [1152], P('tensor'), may hold values from -3 to 3
- mlp_gain: float32 [1152], replicated, may hold values from 0.5 to 1.5
- mlp_shift: float32 [1152], replicated, may hold values from -1.8 to 1.8
- up_weight: bfloat16 [1152, 4304], P('dp', 'tensor'), may hold values from -0.1875 to 0.1875
- up_bias: float32 [4304], P('tensor'), may hold values from -3 to 3
- down_weight: bfloat16 [4304, 1152], P('tensor', 'dp'), may hold values from -0.125 to 0.125
- down_bias: float32 [1152], P('tensor'), may hold values from -3 to 3
- cotangent: bfloat16 [24, 729, 1152], P('dp', None, 'tensor'), may hold values from -6 to 6
Outputs:
- layer_out: bfloat16 [24, 729, 1152], P('dp', None, 'tensor')
- image_grad: bfloat16 [24, 729, 1152], P('dp', None, 'tensor')
- attn_gain_grad: float32 [1152], P('tensor')
- attn_shift_grad: float32 [1152], P('tensor')
- query_weight_grad: float32 [1152, 1152], P('dp', 'tensor')
- query_bias_grad: float32 [1152], P('tensor')
- key_weight_grad: float32 [1152, 1152], P('dp', 'tensor')
- value_weight_grad: float32 [1152, 1152], P('dp', 'tensor')
- value_bias_grad: float32 [1152], P('tensor')
- output_weight_grad: float32 [1152, 1152], P('tensor', 'dp')
- output_bias_grad: float32 [1152], P('tensor')
- mlp_gain_grad: float32 [1152], P('tensor')
- mlp_shift_grad: float32 [1152], P('tensor')
- up_weight_grad: float32 [1152, 4304], P('dp', 'tensor')
- up_bias_grad: float32 [4304], P('tensor')
- down_weight_grad: float32 [4304, 1152], P('tensor', 'dp')
- down_bias_grad: float32 [1152], P('tensor')
Inputs may be any that keep to these rules, and one draw needn't show every extreme that they name: Slots 0 to image_count - 1 of a data position hold its images; some position has 3 images and some has 2.
All inputs are finite; a program needn't handle non-finite values.
Results may differ from a plain program's by a relative error of at most 0.017.
Values may be sent and summed in bfloat16 or wider, within the bound.
No kernel may reach another device: no remote copies, remote signals or barrier semaphores. Data moves between devices by JAX's collectives and lax.ppermute only.
A program may use at most 256 MiB of HBM per device.

v0:
```python
import math
import jax
import jax.numpy as jnp
from jax import lax
from jax.sharding import PartitionSpec as P

HDIM = 72
EPSILON = 1e-06


def gelu_tanh(value):
    return jax.nn.gelu(value, approximate=True)


def fetch_weights(query_weight, key_weight, value_weight, up_weight, output_weight, down_weight):
    row_parts = (
        lax.all_gather(query_weight, "dp", axis=0, tiled=True),
        lax.all_gather(key_weight, "dp", axis=0, tiled=True),
        lax.all_gather(value_weight, "dp", axis=0, tiled=True),
        lax.all_gather(up_weight, "dp", axis=0, tiled=True),
    )
    col_parts = (
        lax.all_gather(output_weight, "dp", axis=1, tiled=True),
        lax.all_gather(down_weight, "dp", axis=1, tiled=True),
    )
    return tuple(row_parts) + tuple(col_parts)


def normalize(rows):
    centred = rows - jnp.mean(rows, axis=1, keepdims=True)
    inverse = lax.rsqrt(jnp.mean(centred * centred, axis=1, keepdims=True) + EPSILON)
    return (centred * inverse, inverse)


def norm_back(grad_share, normed_share, inverse, gain_share):
    scaled = grad_share * gain_share
    totals = lax.psum((jnp.sum(scaled, axis=1), jnp.sum(scaled * normed_share, axis=1)), "tensor")
    width = grad_share.shape[1] * lax.axis_size("tensor")
    first_mean = totals[0][:, None] / width
    second_mean = totals[1][:, None] / width
    return inverse * (scaled - first_mean - normed_share * second_mean)


def split_heads(rows):
    return rows.reshape(rows.shape[0], -1, HDIM).transpose(1, 0, 2)


def merge_heads(blocks):
    return blocks.transpose(1, 0, 2).reshape(blocks.shape[1], -1)


def column_share(whole, start, width):
    return lax.dynamic_slice_in_dim(whole, start, width, whole.ndim - 1)


def local(
    images,
    image_count,
    attn_gain,
    attn_shift,
    query_weight,
    query_bias,
    key_weight,
    value_weight,
    value_bias,
    output_weight,
    output_bias,
    mlp_gain,
    mlp_shift,
    up_weight,
    up_bias,
    down_weight,
    down_bias,
    cotangent,
):
    share_width = images.shape[2]
    share_start = lax.axis_index("tensor") * share_width
    attn_gain_share = column_share(attn_gain, share_start, share_width)
    mlp_gain_share = column_share(mlp_gain, share_start, share_width)
    score_scale = 1.0 / math.sqrt(HDIM)
    grads_sum = None
    out_slots = []
    grad_slots = []
    for slot_index in range(images.shape[0]):
        weights_now = fetch_weights(
            query_weight, key_weight, value_weight, up_weight, output_weight, down_weight
        )
        query_full, key_full, value_full, up_full, output_full, down_full = weights_now
        live_flag = (image_count[0] > slot_index).astype(jnp.float32)
        rows_pair = (
            lax.all_gather(images[slot_index], "tensor", axis=1, tiled=True),
            lax.all_gather(cotangent[slot_index], "tensor", axis=1, tiled=True),
        )
        input_full = rows_pair[0].astype(jnp.float32)
        grad_full = rows_pair[1].astype(jnp.float32) * live_flag
        grad_low = grad_full.astype(jnp.bfloat16)
        input_share = images[slot_index].astype(jnp.float32)
        grad_share = cotangent[slot_index].astype(jnp.float32) * live_flag
        normed1, inverse1 = normalize(input_full)
        attn_in = (normed1 * attn_gain + attn_shift).astype(jnp.bfloat16)
        query_low = (
            jnp.dot(attn_in, query_full, preferred_element_type=jnp.float32) + query_bias
        ).astype(jnp.bfloat16)
        key_low = jnp.dot(attn_in, key_full, preferred_element_type=jnp.float32).astype(
            jnp.bfloat16
        )
        value_low = (
            jnp.dot(attn_in, value_full, preferred_element_type=jnp.float32) + value_bias
        ).astype(jnp.bfloat16)
        query_heads = split_heads(query_low)
        key_heads = split_heads(key_low)
        value_heads = split_heads(value_low)
        scores = (
            jnp.einsum("hqd,hkd->hqk", query_heads, key_heads, preferred_element_type=jnp.float32)
            * score_scale
        )
        row_max = jnp.max(scores, axis=-1, keepdims=True)
        expo = jnp.exp(scores - row_max)
        prob_total = jnp.sum(expo, axis=-1, keepdims=True)
        log_total = row_max + jnp.log(prob_total)
        probs_low = (expo / prob_total).astype(jnp.bfloat16)
        mixed_heads = jnp.einsum(
            "hqk,hkd->hqd", probs_low, value_heads, preferred_element_type=jnp.float32
        )
        mixed_low = merge_heads(mixed_heads).astype(jnp.bfloat16)
        attn_partial = jnp.dot(mixed_low, output_full, preferred_element_type=jnp.float32)
        attn_share = lax.psum_scatter(attn_partial, "tensor", scatter_dimension=1, tiled=True)
        hidden1_share = input_share + attn_share + output_bias
        hidden1_full = lax.all_gather(hidden1_share, "tensor", axis=1, tiled=True)
        normed2, inverse2 = normalize(hidden1_full)
        mlp_in = (normed2 * mlp_gain + mlp_shift).astype(jnp.bfloat16)
        pre_act = jnp.dot(mlp_in, up_full, preferred_element_type=jnp.float32) + up_bias
        activ, gelu_pull = jax.vjp(gelu_tanh, pre_act)
        activ_low = activ.astype(jnp.bfloat16)
        mlp_partial = jnp.dot(activ_low, down_full, preferred_element_type=jnp.float32)
        mlp_share = lax.psum_scatter(
            mlp_partial.astype(jnp.bfloat16), "tensor", scatter_dimension=1, tiled=True
        ).astype(jnp.float32)
        out_slots.append(((hidden1_share + mlp_share + down_bias) * live_flag).astype(jnp.bfloat16))
        down_grad = jnp.einsum("sf,sd->fd", activ_low, grad_low, preferred_element_type=jnp.float32)
        hidden_grad = jnp.einsum(
            "sd,fd->sf", grad_low, down_full, preferred_element_type=jnp.float32
        )
        pre_grad = gelu_pull(hidden_grad)[0].astype(jnp.bfloat16)
        up_grad = jnp.einsum("sd,sf->df", mlp_in, pre_grad, preferred_element_type=jnp.float32)
        norm2_partial = jnp.einsum(
            "sf,df->sd", pre_grad, up_full, preferred_element_type=jnp.float32
        )
        normed2_share = column_share(normed2, share_start, share_width)
        norm2_share = lax.psum_scatter(norm2_partial, "tensor", scatter_dimension=1, tiled=True)
        hidden1_grad = grad_share + norm_back(norm2_share, normed2_share, inverse2, mlp_gain_share)
        branch_low = lax.all_gather(hidden1_grad.astype(jnp.bfloat16), "tensor", axis=1, tiled=True)
        output_grad = jnp.einsum(
            "sh,sd->hd", mixed_low, branch_low, preferred_element_type=jnp.float32
        )
        mixed_grad = split_heads(
            jnp.einsum(
                "sd,hd->sh", branch_low, output_full, preferred_element_type=jnp.float32
            ).astype(jnp.bfloat16)
        )
        scores_again = (
            jnp.einsum("hqd,hkd->hqk", query_heads, key_heads, preferred_element_type=jnp.float32)
            * score_scale
        )
        probs_again = jnp.exp(scores_again - log_total)
        probs_again_low = probs_again.astype(jnp.bfloat16)
        prob_grad = jnp.einsum(
            "hqd,hkd->hqk", mixed_grad, value_heads, preferred_element_type=jnp.float32
        )
        row_delta = jnp.sum(probs_again * prob_grad, axis=-1, keepdims=True)
        score_grad = (probs_again * (prob_grad - row_delta)).astype(jnp.bfloat16)
        query_grad = merge_heads(
            jnp.einsum("hqk,hkd->hqd", score_grad, key_heads, preferred_element_type=jnp.float32)
            * score_scale
        ).astype(jnp.bfloat16)
        key_grad = merge_heads(
            jnp.einsum("hqk,hqd->hkd", score_grad, query_heads, preferred_element_type=jnp.float32)
            * score_scale
        ).astype(jnp.bfloat16)
        value_grad = merge_heads(
            jnp.einsum(
                "hqk,hqd->hkd", probs_again_low, mixed_grad, preferred_element_type=jnp.float32
            )
        ).astype(jnp.bfloat16)
        query_w_grad = jnp.einsum(
            "sd,sh->dh", attn_in, query_grad, preferred_element_type=jnp.float32
        )
        key_w_grad = jnp.einsum("sd,sh->dh", attn_in, key_grad, preferred_element_type=jnp.float32)
        value_w_grad = jnp.einsum(
            "sd,sh->dh", attn_in, value_grad, preferred_element_type=jnp.float32
        )
        norm1_partial = jnp.einsum(
            "sh,dh->sd", query_grad, query_full, preferred_element_type=jnp.float32
        )
        norm1_partial = norm1_partial + jnp.einsum(
            "sh,dh->sd", key_grad, key_full, preferred_element_type=jnp.float32
        )
        norm1_partial = norm1_partial + jnp.einsum(
            "sh,dh->sd", value_grad, value_full, preferred_element_type=jnp.float32
        )
        norm1_share = lax.psum_scatter(
            norm1_partial.astype(jnp.bfloat16), "tensor", scatter_dimension=1, tiled=True
        ).astype(jnp.float32)
        normed1_share = column_share(normed1, share_start, share_width)
        grad_slots.append(
            (
                hidden1_grad + norm_back(norm1_share, normed1_share, inverse1, attn_gain_share)
            ).astype(jnp.bfloat16)
        )
        slot_grads = (
            query_w_grad,
            key_w_grad,
            value_w_grad,
            up_grad,
            output_grad,
            down_grad,
            jnp.sum(norm1_share * normed1_share, axis=0),
            jnp.sum(norm1_share, axis=0),
            jnp.sum(query_grad.astype(jnp.float32), axis=0),
            jnp.sum(value_grad.astype(jnp.float32), axis=0),
            jnp.sum(hidden1_grad, axis=0),
            jnp.sum(norm2_share * normed2_share, axis=0),
            jnp.sum(norm2_share, axis=0),
            jnp.sum(pre_grad.astype(jnp.float32), axis=0),
            jnp.sum(grad_share, axis=0),
        )
        grads_sum = (
            slot_grads if grads_sum is None else jax.tree.map(jnp.add, grads_sum, slot_grads)
        )
    row_grads = (
        lax.psum_scatter(grads_sum[0], "dp", scatter_dimension=0, tiled=True),
        lax.psum_scatter(grads_sum[1], "dp", scatter_dimension=0, tiled=True),
        lax.psum_scatter(grads_sum[2], "dp", scatter_dimension=0, tiled=True),
        lax.psum_scatter(grads_sum[3], "dp", scatter_dimension=0, tiled=True),
    )
    col_grads = (
        lax.psum_scatter(grads_sum[4], "dp", scatter_dimension=1, tiled=True),
        lax.psum_scatter(grads_sum[5], "dp", scatter_dimension=1, tiled=True),
    )
    small = lax.psum(
        (
            grads_sum[6],
            grads_sum[7],
            grads_sum[8],
            grads_sum[9],
            grads_sum[10],
            grads_sum[11],
            grads_sum[12],
            grads_sum[13],
            grads_sum[14],
        ),
        "dp",
    )
    return (
        jnp.stack(out_slots),
        jnp.stack(grad_slots),
        small[0],
        small[1],
        row_grads[0],
        small[2],
        row_grads[1],
        row_grads[2],
        small[3],
        col_grads[0],
        small[4],
        small[5],
        small[6],
        row_grads[3],
        small[7],
        col_grads[1],
        small[8],
    )


def solution(mesh):
    in_specs = (
        P("dp", None, "tensor"),
        P("dp"),
        P(),
        P(),
        P("dp", "tensor"),
        P("tensor"),
        P("dp", "tensor"),
        P("dp", "tensor"),
        P("tensor"),
        P("tensor", "dp"),
        P("tensor"),
        P(),
        P(),
        P("dp", "tensor"),
        P("tensor"),
        P("tensor", "dp"),
        P("tensor"),
        P("dp", None, "tensor"),
    )
    out_specs = (
        P("dp", None, "tensor"),
        P("dp", None, "tensor"),
        P("tensor"),
        P("tensor"),
        P("dp", "tensor"),
        P("tensor"),
        P("dp", "tensor"),
        P("dp", "tensor"),
        P("tensor"),
        P("tensor", "dp"),
        P("tensor"),
        P("tensor"),
        P("tensor"),
        P("dp", "tensor"),
        P("tensor"),
        P("tensor", "dp"),
        P("tensor"),
    )
    return jax.shard_map(local, mesh=mesh, in_specs=in_specs, out_specs=out_specs, check_vma=False)
```

profile of v0, /device:TPU:0, one launch (start us, length us, event | category | flops | bytes accessed | tf_op | source)
XLA Modules:
  0.0 1480.5 jit_solution(229131202090913659)
XLA Ops:
  11.3 34.3 %all_gather.67 = bf16[1152,288]{1,0:T(8,128)(2,1)S(1)} all-gather(bf16[144,288]{1,0:T(8,128)(2,1)S(1)} %copy-done.91), channel_id=1, replica_groups=mesh['dp'=8,'tensor'=4] {'dp'}, dimensions={0}, use_global_device_ids=true | all-gather | bytes 746496 | tf_op jit(solution)/shard_map/all_gather | solution.py:17
  45.6 32.7 %all_gather.68 = bf16[1152,288]{1,0:T(8,128)(2,1)S(1)} all-gather(bf16[144,288]{1,0:T(8,128)(2,1)S(1)} %copy-done.92), channel_id=1, replica_groups=mesh['dp'=8,'tensor'=4] {'dp'}, dimensions={0}, use_global_device_ids=true | all-gather | bytes 746496 | tf_op jit(solution)/shard_map/all_gather | solution.py:18
  78.3 32.3 %all_gather.69 = bf16[1152,288]{1,0:T(8,128)(2,1)S(1)} all-gather(bf16[144,288]{1,0:T(8,128)(2,1)S(1)} %copy-done.93), channel_id=1, replica_groups=mesh['dp'=8,'tensor'=4] {'dp'}, dimensions={0}, use_global_device_ids=true | all-gather | bytes 746496 | tf_op jit(solution)/shard_map/all_gather | solution.py:19
  110.6 32.1 %all_gather.70 = bf16[288,1152]{0,1:T(8,128)(2,1)S(1)} all-gather(bf16[288,144]{0,1:T(8,128)(2,1)} %param.27), channel_id=1, replica_groups=mesh['dp'=8,'tensor'=4] {'dp'}, dimensions={1}, use_global_device_ids=true | all-gather | bytes 746496 | tf_op jit(solution)/shard_map/all_gather | solution.py:23
  204.2 43.1 %reduce-scatter.27.cloned.1.call-done = f32[729,288]{0,1:T(8,128)} async-done(((f32[729,1152]{0,1:T(8,128)}), f32[729,288]{0,1:T(8,128)}) %reduce-scatter.27.cloned.1.call-update) | async-done | bytes 839824 | tf_op jit(solution)/shard_map/reduce_scatter | solution.py:127
  247.3 42.9 %reduce-scatter.19.cloned.1.call-done = f32[729,288]{0,1:T(8,128)} async-done(((f32[729,1152]{0,1:T(8,128)}), f32[729,288]{0,1:T(8,128)}) %reduce-scatter.19.cloned.1.call-update) | async-done | bytes 839824 | tf_op jit(solution)/shard_map/reduce_scatter | solution.py:127
  299.8 24.9 %all-gather.29.cloned.1.call-done = f32[729,1152]{0,1:T(8,128)} async-done(((f32[729,288]{0,1:T(8,128)}), f32[729,1152]{0,1:T(8,128)}) %all-gather.29.cloned.1.call-update) | async-done | bytes 3359248 | tf_op jit(solution)/shard_map/all_gather | solution.py:129
  330.3 51.8 %all-gather.23.cloned.1.call-done = bf16[1152,1076]{1,0:T(8,128)(2,1)} async-done(((bf16[144,1076]{1,0:T(8,128)(2,1)}), bf16[1152,1076]{1,0:T(8,128)(2,1)}) %all-gather.23.cloned.1.call-update) | async-done | bytes 2479120 | tf_op jit(solution)/shard_map/all_gather | solution.py:20
  387.6 16.2 %all-gather.47.cloned.1.call-done = bf16[1,729,1152]{1,2,0:T(8,128)(2,1)} async-done(((bf16[1,729,288]{1,2,0:T(8,128)(2,1)}), bf16[1,729,1152]{1,2,0:T(8,128)(2,1)}) %all-gather.47.cloned.1.call-update) | async-done | bytes 1679632 | tf_op jit(solution)/shard_map/all_gather | solution.py:92
  403.7 57.3 %all-gather.25.cloned.1.call-done = bf16[1076,1152]{0,1:T(8,128)(2,1)} async-done(((bf16[1076,144]{0,1:T(8,128)(2,1)}), bf16[1076,1152]{0,1:T(8,128)(2,1)}) %all-gather.25.cloned.1.call-update) | async-done | bytes 2479120 | tf_op jit(solution)/shard_map/all_gather | solution.py:24
  474.5 18.2 %all-gather.27.cloned.1.call-done = f32[729,1152]{0,1:T(8,128)} async-done(((f32[729,288]{0,1:T(8,128)}), f32[729,1152]{0,1:T(8,128)}) %all-gather.27.cloned.1.call-update) | async-done | bytes 3359248 | tf_op jit(solution)/shard_map/all_gather | solution.py:129
  503.4 11.6 all-gather.45.cloned.1.call-done
  528.4 19.5 %all-gather.21.cloned.1.call-done = f32[729,1152]{0,1:T(8,128)} async-done(((f32[729,288]{0,1:T(8,128)}), f32[729,1152]{0,1:T(8,128)}) %all-gather.21.cloned.1.call-update) | async-done | bytes 3359248 | tf_op jit(solution)/shard_map/all_gather | solution.py:129
  558.9 12.0 all-gather.43.cloned.1.call-done
  585.0 28.9 %reduce-scatter.39.cloned.1.call-done = f32[729,288]{0,1:T(8,128)} async-done(((f32[729,1152]{0,1:T(8,128)}), f32[729,288]{0,1:T(8,128)}) %reduce-scatter.39.cloned.1.call-update) | async-done | bytes 839824 | tf_op jit(solution)/shard_map/reduce_scatter | solution.py:150
  613.9 42.9 %reduce-scatter.35.cloned.1.call-done = f32[729,288]{0,1:T(8,128)} async-done(((f32[729,1152]{0,1:T(8,128)}), f32[729,288]{0,1:T(8,128)}) %reduce-scatter.35.cloned.1.call-update) | async-done | bytes 839824 | tf_op jit(solution)/shard_map/reduce_scatter | solution.py:150
  656.7 43.0 %reduce-scatter.31.cloned.1.call-done = f32[729,288]{0,1:T(8,128)} async-done(((f32[729,1152]{0,1:T(8,128)}), f32[729,288]{0,1:T(8,128)}) %reduce-scatter.31.cloned.1.call-update) | async-done | bytes 839824 | tf_op jit(solution)/shard_map/reduce_scatter | solution.py:150
  703.8 10.5 all-reduce.2
  755.4 10.2 multiply_convert_fusion.2
  782.8 7.7 multiply_reduce_fusion
  790.5 10.8 multiply_convert_fusion
  825.1 11.1 multiply_convert_fusion.1
  919.0 27.4 %reduce-scatter.41.cloned.1.call-done = bf16[729,288]{0,1:T(8,128)(2,1)} async-done(((bf16[729,1152]{0,1:T(8,128)(2,1)}), bf16[729,288]{0,1:T(8,128)(2,1)}) %reduce-scatter.41.cloned.1.call-update) | async-done | bytes 419920 | tf_op jit(solution)/shard_map/reduce_scatter | solution.py:201
  946.4 32.0 %reduce-scatter.37.cloned.1.call-done = bf16[729,288]{0,1:T(8,128)(2,1)} async-done(((bf16[729,1152]{0,1:T(8,128)(2,1)}), bf16[729,288]{0,1:T(8,128)(2,1)}) %reduce-scatter.37.cloned.1.call-update) | async-done | bytes 419920 | tf_op jit(solution)/shard_map/reduce_scatter | solution.py:201
  983.4 40.5 %all-reduce = (f32[288]{0:T(512)}, f32[288]{0:T(512)}, f32[288]{0:T(512)}, f32[288]{0:T(512)}, f32[288]{0:T(512)}, /*index=5*/f32[288]{0:T(512)}, f32[288]{0:T(512)}, f32[1076]{0:T(1024)}, f32[288]{0:T(512)}) all-reduce(f32[288]{0:T(512)} %add_add_fusion.8, f32[288]{0:T(512)} %add_add_fusion.7, ...), channel_id=1, replica_groups=mesh['dp'=8,'tensor'=4] {'dp'}, use_global_device_ids=true, to_apply=%region_60.0 | all-reduce | flops 3380 | bytes 27040 | tf_op jit(solution)/shard_map/psum | solution.py:240
  1023.9 12.2 all-reduce.1
  1045.0 42.1 %reduce-scatter.53.cloned.1.call-done = f32[1076,144]{0,1:T(8,128)} async-done(((f32[1076,1152]{0,1:T(8,128)}), f32[1076,144]{0,1:T(8,128)}) %reduce-scatter.53.cloned.1.call-update) | async-done | bytes 619792 | tf_op jit(solution)/shard_map/reduce_scatter | solution.py:238
  1087.2 108.6 %reduce-scatter.51.cloned.1.call-done = f32[144,1076]{1,0:T(8,128)} async-done(((f32[1152,1076]{1,0:T(8,128)}), f32[144,1076]{1,0:T(8,128)}) %reduce-scatter.51.cloned.1.call-update) | async-done | bytes 619792 | tf_op jit(solution)/shard_map/reduce_scatter | solution.py:234
  1195.7 69.7 %reduce-scatter.49.cloned.1.call-done = f32[288,144]{0,1:T(8,128)} async-done(((f32[288,1152]{0,1:T(8,128)}), f32[288,144]{0,1:T(8,128)}) %reduce-scatter.49.cloned.1.call-update) | async-done | bytes 165904 | tf_op jit(solution)/shard_map/reduce_scatter | solution.py:237
  1265.5 69.7 %reduce-scatter.47.cloned.1.call-done = f32[144,288]{1,0:T(8,128)} async-done(((f32[1152,288]{1,0:T(8,128)}), f32[144,288]{1,0:T(8,128)}) %reduce-scatter.47.cloned.1.call-update) | async-done | bytes 165904 | tf_op jit(solution)/shard_map/reduce_scatter | solution.py:233
  1335.2 69.2 %reduce-scatter.43.cloned.1.call-done = f32[144,288]{1,0:T(8,128)} async-done(((f32[1152,288]{1,0:T(8,128)}), f32[144,288]{1,0:T(8,128)}) %reduce-scatter.43.cloned.1.call-update) | async-done | bytes 165904 | tf_op jit(solution)/shard_map/reduce_scatter | solution.py:231
  1404.3 69.4 %reduce-scatter.45.cloned.1.call-done = f32[144,288]{1,0:T(8,128)} async-done(((f32[1152,288]{1,0:T(8,128)}), f32[144,288]{1,0:T(8,128)}) %reduce-scatter.45.cloned.1.call-update) | async-done | bytes 165904 | tf_op jit(solution)/shard_map/reduce_scatter | solution.py:232
  (542 shorter events, 328.8 us)
Async XLA Ops:
  7.2 135.5 %all-gather.39.cloned.1.call-start = ((), (), s32[]{:S(2)}) async-start(), calls=%async_computation.45 | async-start | bytes 2211840 | tf_op jit(solution)/shard_map/all_gather | solution.py:91
  9.7 152.9 %all-gather.41.cloned.1.call-start = ((), (), s32[]{:S(2)}) async-start(), calls=%async_computation.46 | async-start | bytes 2211840 | tf_op jit(solution)/shard_map/all_gather | solution.py:91
  10.5 172.1 %all-gather.37.cloned.1.call-start = ((), (), s32[]{:S(2)}) async-start(), calls=%async_computation.44 | async-start | bytes 2211840 | tf_op jit(solution)/shard_map/all_gather | solution.py:91
  11.2 193.0 %reduce-scatter.23.cloned.1.call-start = ((), (), s32[]{:S(2)}) async-start(), calls=%async_computation.23 | async-start | bytes 4423680 | tf_op jit(solution)/shard_map/reduce_scatter | solution.py:127
  162.1 85.2 %reduce-scatter.27.cloned.1.call-start = ((), (), s32[]{:S(2)}) async-start(), calls=%async_computation.26 | async-start | bytes 4423680 | tf_op jit(solution)/shard_map/reduce_scatter | solution.py:127
  182.4 107.8 %reduce-scatter.19.cloned.1.call-start = ((), (), s32[]{:S(2)}) async-start(), calls=%async_computation.18 | async-start | bytes 4423680 | tf_op jit(solution)/shard_map/reduce_scatter | solution.py:127
  202.4 122.3 %all-gather.29.cloned.1.call-start = ((), (), s32[]{:S(2)}) async-start(), calls=%async_computation.27 | async-start | bytes 4423680 | tf_op jit(solution)/shard_map/all_gather | solution.py:129
  293.8 88.4 %all-gather.23.cloned.1.call-start = ((), (), s32[]{:S(2)}) async-start(), calls=%async_computation.20 | async-start | bytes 2985984 | tf_op jit(solution)/shard_map/all_gather | solution.py:20
  294.5 109.2 %all-gather.47.cloned.1.call-start = ((), (), s32[]{:S(2)}) async-start(), calls=%async_computation.49 | async-start | bytes 2211840 | tf_op jit(solution)/shard_map/all_gather | solution.py:92
  295.7 165.4 %all-gather.25.cloned.1.call-start = ((), (), s32[]{:S(2)}) async-start(), calls=%async_computation.21 | async-start | bytes 2985984 | tf_op jit(solution)/shard_map/all_gather | solution.py:24
  296.3 196.4 %all-gather.27.cloned.1.call-start = ((), (), s32[]{:S(2)}) async-start(), calls=%async_computation.24 | async-start | bytes 4423680 | tf_op jit(solution)/shard_map/all_gather | solution.py:129
  297.0 217.9 %all-gather.45.cloned.1.call-start = ((), (), s32[]{:S(2)}) async-start(), calls=%async_computation.48 | async-start | bytes 2211840 | tf_op jit(solution)/shard_map/all_gather | solution.py:92
  297.6 250.4 %all-gather.21.cloned.1.call-start = ((), (), s32[]{:S(2)}) async-start(), calls=%async_computation.19 | async-start | bytes 4423680 | tf_op jit(solution)/shard_map/all_gather | solution.py:129
  298.3 272.5 %all-gather.43.cloned.1.call-start = ((), (), s32[]{:S(2)}) async-start(), calls=%async_computation.47 | async-start | bytes 2211840 | tf_op jit(solution)/shard_map/all_gather | solution.py:92
  298.9 314.9 %reduce-scatter.39.cloned.1.call-start = ((), (), s32[]{:S(2)}) async-start(), calls=%async_computation.35 | async-start | bytes 4423680 | tf_op jit(solution)/shard_map/reduce_scatter | solution.py:150
  474.0 182.7 %reduce-scatter.35.cloned.1.call-start = ((), (), s32[]{:S(2)}) async-start(), calls=%async_computation.32 | async-start | bytes 4423680 | tf_op jit(solution)/shard_map/reduce_scatter | solution.py:150
  528.2 171.6 %reduce-scatter.31.cloned.1.call-start = ((), (), s32[]{:S(2)}) async-start(), calls=%async_computation.29 | async-start | bytes 4423680 | tf_op jit(solution)/shard_map/reduce_scatter | solution.py:150
  584.0 161.5 %all-gather.31.cloned.1.call-start = ((), (), s32[]{:S(2)}) async-start(), calls=%async_computation.30 | async-start | bytes 2211840 | tf_op jit(solution)/shard_map/all_gather | solution.py:152
  719.1 61.3 %all-gather.35.cloned.1.call-start = ((), (), s32[]{:S(2)}) async-start(), calls=%async_computation.36 | async-start | bytes 2211840 | tf_op jit(solution)/shard_map/all_gather | solution.py:152
  720.0 95.8 %all-gather.33.cloned.1.call-start = ((), (), s32[]{:S(2)}) async-start(), calls=%async_computation.33 | async-start | bytes 2211840 | tf_op jit(solution)/shard_map/all_gather | solution.py:152
  724.0 179.7 %reduce-scatter.21.cloned.1.call-start = ((), (), s32[]{:S(2)}) async-start(), calls=%async_computation.22 | async-start | bytes 2211840 | tf_op jit(solution)/shard_map/reduce_scatter | solution.py:136
  730.8 172.8 %reduce-scatter.25.cloned.1.call-start = ((), (), s32[]{:S(2)}) async-start(), calls=%async_computation.25 | async-start | bytes 2211840 | tf_op jit(solution)/shard_map/reduce_scatter | solution.py:136
  737.5 166.2 %reduce-scatter.29.cloned.1.call-start = ((), (), s32[]{:S(2)}) async-start(), calls=%async_computation.28 | async-start | bytes 2211840 | tf_op jit(solution)/shard_map/reduce_scatter | solution.py:136
  745.1 173.9 %reduce-scatter.33.cloned.1.call-start = ((), (), s32[]{:S(2)}) async-start(), calls=%async_computation.31 | async-start | bytes 2211840 | tf_op jit(solution)/shard_map/reduce_scatter | solution.py:201
  780.1 166.3 %reduce-scatter.41.cloned.1.call-start = ((), (), s32[]{:S(2)}) async-start(), calls=%async_computation.37 | async-start | bytes 2211840 | tf_op jit(solution)/shard_map/reduce_scatter | solution.py:201
  815.4 163.0 %reduce-scatter.37.cloned.1.call-start = ((), (), s32[]{:S(2)}) async-start(), calls=%async_computation.34 | async-start | bytes 2211840 | tf_op jit(solution)/shard_map/reduce_scatter | solution.py:201
  850.3 236.9 %reduce-scatter.53.cloned.1.call-start = ((), (), s32[]{:S(2)}) async-start(), calls=%async_computation.43 | async-start | bytes 5971968 | tf_op jit(solution)/shard_map/reduce_scatter | solution.py:238
  863.6 332.2 %reduce-scatter.51.cloned.1.call-start = ((), (), s32[]{:S(2)}) async-start(), calls=%async_computation.42 | async-start | bytes 5971968 | tf_op jit(solution)/shard_map/reduce_scatter | solution.py:234
  877.9 387.6 %reduce-scatter.49.cloned.1.call-start = ((), (), s32[]{:S(2)}) async-start(), calls=%async_computation.41 | async-start | bytes 1990656 | tf_op jit(solution)/shard_map/reduce_scatter | solution.py:237
  885.5 449.7 %reduce-scatter.47.cloned.1.call-start = ((), (), s32[]{:S(2)}) async-start(), calls=%async_computation.40 | async-start | bytes 1990656 | tf_op jit(solution)/shard_map/reduce_scatter | solution.py:233
  892.8 511.6 %reduce-scatter.43.cloned.1.call-start = ((), (), s32[]{:S(2)}) async-start(), calls=%async_computation.38 | async-start | bytes 1990656 | tf_op jit(solution)/shard_map/reduce_scatter | solution.py:231
  902.3 571.5 %reduce-scatter.45.cloned.1.call-start = ((), (), s32[]{:S(2)}) async-start(), calls=%async_computation.39 | async-start | bytes 1990656 | tf_op jit(solution)/shard_map/reduce_scatter | solution.py:232
  (160 other events, 2436.1 us)
Sparse Core Ops, SparseCore 0:
  10.2 23.4 all-gather.38
  35.8 20.7 all-gather.40
  58.7 20.7 all-gather.36
  162.2 41.9 reduce-scatter.22
  206.8 40.4 reduce-scatter.26
  249.7 40.4 reduce-scatter.18
  293.9 30.7 all-gather.28
  327.1 55.0 all-gather.22
  384.4 19.3 all-gather.46
  406.0 55.0 all-gather.24
  463.3 29.3 all-gather.26
  494.1 20.7 all-gather.44
  517.1 30.7 all-gather.20
  550.0 20.7 all-gather.42
  573.4 40.4 reduce-scatter.38
  616.3 40.4 reduce-scatter.34
  659.3 40.4 reduce-scatter.30
  719.2 21.8 all-gather.30
  743.2 20.7 all-gather.34
  765.4 20.7 all-gather.32
  788.8 29.4 reduce-scatter.20
  821.1 29.3 reduce-scatter.24
  853.0 29.3 reduce-scatter.28
  885.0 29.3 reduce-scatter.32
  917.0 29.3 reduce-scatter.40
  949.0 29.3 reduce-scatter.36
  982.5 104.6 reduce-scatter.52
  1091.8 103.9 reduce-scatter.50
  1199.8 65.6 reduce-scatter.48
  1269.8 65.3 reduce-scatter.46
  1339.2 65.0 reduce-scatter.42
  1408.8 64.9 reduce-scatter.44
where the time goes:
time: 1490 us; the launch traced here: 1480 us
  waiting for transfers between devices  908 us (61%)
  matrix products  214 us (14%)
  blocking collectives  195 us (13%)
  other arithmetic  108 us (7%)
  local copies, waits for them, and re-layouts  34.3 us (2%)
  between operations  17 us (1%)
    reduce_scatter x3, waiting for transfers between devices, local(): lax.psum_scatter(norm2_partial, 'tensor', scatter_dimension=1, tiled=True)  115 us
    reduce_scatter x1, waiting for transfers between devices, local(): lax.psum_scatter(grads_sum[3], 'dp', scatter_dimension=0, tiled=True)  109 us
    reduce_scatter x3, waiting for transfers between devices, local(): lax.psum_scatter(attn_partial, 'tensor', scatter_dimension=1, tiled=True)  87.7 us
    reduce_scatter x1, waiting for transfers between devices, local(): lax.psum_scatter(grads_sum[4], 'dp', scatter_dimension=1, tiled=True)  69.7 us
    reduce_scatter x1, waiting for transfers between devices, local(): lax.psum_scatter(grads_sum[2], 'dp', scatter_dimension=0, tiled=True)  69.7 us
    reduce_scatter x1, waiting for transfers between devices, local(): lax.psum_scatter(grads_sum[1], 'dp', scatter_dimension=0, tiled=True)  69.4 us
    reduce_scatter x1, waiting for transfers between devices, local(): lax.psum_scatter(grads_sum[0], 'dp', scatter_dimension=0, tiled=True)  69.2 us
    all_gather x3, waiting for transfers between devices, local(): hidden1_full = lax.all_gather(hidden1_share, 'tensor', axis=1, tiled=True)  62.6 us
  transfers between devices with their start and end apart: 32, of which 22 were waited for; matrix products, arithmetic and copies ran while one was open for 21% of the time, Pallas kernels for 0%

commit v1 on v0

--- a/solution.py
+++ b/solution.py
@@ -13,11 +13,26 @@
 
 
 def fetch_weights(query_weight, key_weight, value_weight, up_weight, output_weight, down_weight):
+
+    def wall_recover(incoming_x, bus_axis):
+        devs = lax.axis_size(bus_axis)
+        ledger = [(u, (u + 1) % devs) for u in range(devs)]
+        long_array, after = ([incoming_x], [incoming_x])
+        column = [(u, (u - 1) % devs) for u in range(devs)]
+        for _ in range(devs // 2):
+            long_array.append(lax.ppermute(long_array[-1], bus_axis, ledger))
+        for _ in range((devs - 1) // 2):
+            after.append(lax.ppermute(after[-1], bus_axis, column))
+        placed = jnp.concatenate([*long_array[::-1], *after[1:]], axis=0)
+        return jnp.roll(
+            placed, (lax.axis_index(bus_axis) - devs // 2) * incoming_x.shape[0], axis=0
+        )
+
     row_parts = (
         lax.all_gather(query_weight, "dp", axis=0, tiled=True),
         lax.all_gather(key_weight, "dp", axis=0, tiled=True),
         lax.all_gather(value_weight, "dp", axis=0, tiled=True),
-        lax.all_gather(up_weight, "dp", axis=0, tiled=True),
+        wall_recover(up_weight, "dp"),
     )
     col_parts = (
         lax.all_gather(output_weight, "dp", axis=1, tiled=True),

time: 1490 us -> 1430 us (0.960)
  waiting for transfers between devices: 908 us -> 820 us
  starting transfers between devices: 4.31 us -> 32.5 us
    all_gather x1 -> x0, waiting for transfers between devices: 51.8 us -> none  [fetch_weights(): lax.all_gather(up_weight, 'dp', axis=0, tiled=True)]
    ppermute x0 -> x7, waiting for transfers between devices: none -> 30.4 us  [the longest x4 27 us: wall_recover(): long_array.append(lax.ppermute(long_array[-1], bus_axis, ledger))]
    ppermute x0 -> x7, starting transfers between devices: none -> 28.9 us  [the longest x3 22.4 us: wall_recover(): after.append(lax.ppermute(after[-1], bus_axis, column))]
    all_gather x3, waiting for transfers between devices: 62.6 us -> 37.4 us  [local(): hidden1_full = lax.all_gather(hidden1_share, 'tensor', axis=1, tiled=True)]
    all_gather x1, waiting for transfers between devices: 57.3 us -> 32.6 us  [fetch_weights(): lax.all_gather(down_weight, 'dp', axis=1, tiled=True)]
    all_gather x3, waiting for transfers between devices: 39.7 us -> 24 us  [local(): lax.all_gather(cotangent[slot_index], 'tensor', axis=1, tiled=True)]
    unnamed x320 -> x337, local copies, waits for them, and re-layouts: 27.7 us -> 30.2 us
  transfers between devices with their start and end apart: 32 -> 38, of which waited for: 22 -> 24; matrix products, arithmetic and copies ran while one was open for 21% -> 22% of each run, Pallas kernels for 0% -> 0%
where the time goes in v1:
time: 1430 us; the launch traced here: 1420 us
  waiting for transfers between devices  820 us (57%)
  matrix products  212 us (15%)
  blocking collectives  195 us (14%)
  other arithmetic  112 us (8%)
  local copies, waits for them, and re-layouts  36.8 us (3%)
  starting transfers between devices  32.5 us (2%)
  between operations  17.4 us (1%)
    reduce_scatter x3, waiting for transfers between devices, local(): lax.psum_scatter(norm2_partial, 'tensor', scatter_dimension=1, tiled=True)  115 us
    reduce_scatter x1, waiting for transfers between devices, local(): lax.psum_scatter(grads_sum[3], 'dp', scatter_dimension=0, tiled=True)  108 us
    reduce_scatter x3, waiting for transfers between devices, local(): lax.psum_scatter(attn_partial, 'tensor', scatter_dimension=1, tiled=True)  88 us
    reduce_scatter x1, waiting for transfers between devices, local(): lax.psum_scatter(grads_sum[4], 'dp', scatter_dimension=1, tiled=True)  70.2 us
    reduce_scatter x1, waiting for transfers between devices, local(): lax.psum_scatter(grads_sum[2], 'dp', scatter_dimension=0, tiled=True)  69.6 us
    reduce_scatter x1, waiting for transfers between devices, local(): lax.psum_scatter(grads_sum[1], 'dp', scatter_dimension=0, tiled=True)  69.3 us
    reduce_scatter x1, waiting for transfers between devices, local(): lax.psum_scatter(grads_sum[0], 'dp', scatter_dimension=0, tiled=True)  69.1 us
    reduce_scatter x3, waiting for transfers between devices, local(): lax.psum_scatter(norm1_partial.astype(jnp.bfloat16), 'tensor', scatter_di...  59.7 us
  transfers between devices with their start and end apart: 38, of which 24 were waited for; matrix products, arithmetic and copies ran while one was open for 22% of the time, Pallas kernels for 0%

profile of v1, /device:TPU:0, one launch (start us, length us, event | category | flops | bytes accessed | tf_op | source)
XLA Modules:
  0.0 1424.7 jit_solution(10284635923003014807)
XLA Ops:
  11.3 34.3 %all_gather.62 = bf16[1152,288]{1,0:T(8,128)(2,1)S(1)} all-gather(bf16[144,288]{1,0:T(8,128)(2,1)S(1)} %copy-done.99), channel_id=1, replica_groups=mesh['dp'=8,'tensor'=4] {'dp'}, dimensions={0}, use_global_device_ids=true | all-gather | bytes 746496 | tf_op jit(solution)/shard_map/all_gather | solution.py:32
  45.6 32.7 %all_gather.63 = bf16[1152,288]{1,0:T(8,128)(2,1)S(1)} all-gather(bf16[144,288]{1,0:T(8,128)(2,1)S(1)} %copy-done.100), channel_id=1, replica_groups=mesh['dp'=8,'tensor'=4] {'dp'}, dimensions={0}, use_global_device_ids=true | all-gather | bytes 746496 | tf_op jit(solution)/shard_map/all_gather | solution.py:33
  78.3 32.3 %all_gather.64 = bf16[1152,288]{1,0:T(8,128)(2,1)S(1)} all-gather(bf16[144,288]{1,0:T(8,128)(2,1)S(1)} %copy-done.101), channel_id=1, replica_groups=mesh['dp'=8,'tensor'=4] {'dp'}, dimensions={0}, use_global_device_ids=true | all-gather | bytes 746496 | tf_op jit(solution)/shard_map/all_gather | solution.py:34
  110.6 32.1 %all_gather.65 = bf16[288,1152]{0,1:T(8,128)(2,1)S(1)} all-gather(bf16[288,144]{0,1:T(8,128)(2,1)} %param.29), channel_id=1, replica_groups=mesh['dp'=8,'tensor'=4] {'dp'}, dimensions={1}, use_global_device_ids=true | all-gather | bytes 746496 | tf_op jit(solution)/shard_map/all_gather | solution.py:38
  204.2 43.1 %reduce-scatter.27.cloned.1.call-done = f32[729,288]{0,1:T(8,128)} async-done(((f32[729,1152]{0,1:T(8,128)}), f32[729,288]{0,1:T(8,128)}) %reduce-scatter.27.cloned.1.call-update) | async-done | bytes 839824 | tf_op jit(solution)/shard_map/reduce_scatter | solution.py:142
  247.2 42.9 %reduce-scatter.19.cloned.1.call-done = f32[729,288]{0,1:T(8,128)} async-done(((f32[729,1152]{0,1:T(8,128)}), f32[729,288]{0,1:T(8,128)}) %reduce-scatter.19.cloned.1.call-update) | async-done | bytes 839824 | tf_op jit(solution)/shard_map/reduce_scatter | solution.py:142
  299.1 10.8 collective-permute-done
  314.6 8.9 collective-permute-done.1
  325.9 8.3 collective-permute-start.5
  342.1 9.4 collective-permute-start.6
  372.5 32.6 %all-gather.22.cloned.1.call-done = bf16[1076,1152]{0,1:T(8,128)(2,1)} async-done(((bf16[1076,144]{0,1:T(8,128)(2,1)}), bf16[1076,1152]{0,1:T(8,128)(2,1)}) %all-gather.22.cloned.1.call-update) | async-done | bytes 2479120 | tf_op jit(solution)/shard_map/all_gather | solution.py:39
  418.4 18.2 %all-gather.24.cloned.1.call-done = f32[729,1152]{0,1:T(8,128)} async-done(((f32[729,288]{0,1:T(8,128)}), f32[729,1152]{0,1:T(8,128)}) %all-gather.24.cloned.1.call-update) | async-done | bytes 3359248 | tf_op jit(solution)/shard_map/all_gather | solution.py:144
  447.3 11.7 all-gather.42.cloned.1.call-done
  472.7 19.2 %all-gather.20.cloned.1.call-done = f32[729,1152]{0,1:T(8,128)} async-done(((f32[729,288]{0,1:T(8,128)}), f32[729,1152]{0,1:T(8,128)}) %all-gather.20.cloned.1.call-update) | async-done | bytes 3359248 | tf_op jit(solution)/shard_map/all_gather | solution.py:144
  502.6 12.3 all-gather.40.cloned.1.call-done
  529.1 28.9 %reduce-scatter.39.cloned.1.call-done = f32[729,288]{0,1:T(8,128)} async-done(((f32[729,1152]{0,1:T(8,128)}), f32[729,288]{0,1:T(8,128)}) %reduce-scatter.39.cloned.1.call-update) | async-done | bytes 839824 | tf_op jit(solution)/shard_map/reduce_scatter | solution.py:165
  558.0 42.9 %reduce-scatter.35.cloned.1.call-done = f32[729,288]{0,1:T(8,128)} async-done(((f32[729,1152]{0,1:T(8,128)}), f32[729,288]{0,1:T(8,128)}) %reduce-scatter.35.cloned.1.call-update) | async-done | bytes 839824 | tf_op jit(solution)/shard_map/reduce_scatter | solution.py:165
  600.8 43.0 %reduce-scatter.31.cloned.1.call-done = f32[729,288]{0,1:T(8,128)} async-done(((f32[729,1152]{0,1:T(8,128)}), f32[729,288]{0,1:T(8,128)}) %reduce-scatter.31.cloned.1.call-update) | async-done | bytes 839824 | tf_op jit(solution)/shard_map/reduce_scatter | solution.py:165
  647.9 10.5 all-reduce.2
  699.3 10.2 multiply_convert_fusion.2
  734.6 10.9 multiply_convert_fusion
  769.2 11.0 multiply_convert_fusion.1
  862.9 27.5 %reduce-scatter.41.cloned.1.call-done = bf16[729,288]{0,1:T(8,128)(2,1)} async-done(((bf16[729,1152]{0,1:T(8,128)(2,1)}), bf16[729,288]{0,1:T(8,128)(2,1)}) %reduce-scatter.41.cloned.1.call-update) | async-done | bytes 419920 | tf_op jit(solution)/shard_map/reduce_scatter | solution.py:216
  890.4 32.2 %reduce-scatter.37.cloned.1.call-done = bf16[729,288]{0,1:T(8,128)(2,1)} async-done(((bf16[729,1152]{0,1:T(8,128)(2,1)}), bf16[729,288]{0,1:T(8,128)(2,1)}) %reduce-scatter.37.cloned.1.call-update) | async-done | bytes 419920 | tf_op jit(solution)/shard_map/reduce_scatter | solution.py:216
  927.5 40.5 %all-reduce = (f32[288]{0:T(512)}, f32[288]{0:T(512)}, f32[288]{0:T(512)}, f32[288]{0:T(512)}, f32[288]{0:T(512)}, /*index=5*/f32[288]{0:T(512)}, f32[288]{0:T(512)}, f32[1076]{0:T(1024)}, f32[288]{0:T(512)}) all-reduce(f32[288]{0:T(512)} %add_add_fusion.8, f32[288]{0:T(512)} %add_add_fusion.7, ...), channel_id=1, replica_groups=mesh['dp'=8,'tensor'=4] {'dp'}, use_global_device_ids=true, to_apply=%region_60.62 | all-reduce | flops 3380 | bytes 27040 | tf_op jit(solution)/shard_map/psum | solution.py:255
  968.0 12.2 all-reduce.1
  989.1 42.0 %reduce-scatter.53.cloned.1.call-done = f32[1076,144]{0,1:T(8,128)} async-done(((f32[1076,1152]{0,1:T(8,128)}), f32[1076,144]{0,1:T(8,128)}) %reduce-scatter.53.cloned.1.call-update) | async-done | bytes 619792 | tf_op jit(solution)/shard_map/reduce_scatter | solution.py:253
  1031.1 108.4 %reduce-scatter.51.cloned.1.call-done = f32[144,1076]{1,0:T(8,128)} async-done(((f32[1152,1076]{1,0:T(8,128)}), f32[144,1076]{1,0:T(8,128)}) %reduce-scatter.51.cloned.1.call-update) | async-done | bytes 619792 | tf_op jit(solution)/shard_map/reduce_scatter | solution.py:249
  1139.5 70.2 %reduce-scatter.49.cloned.1.call-done = f32[288,144]{0,1:T(8,128)} async-done(((f32[288,1152]{0,1:T(8,128)}), f32[288,144]{0,1:T(8,128)}) %reduce-scatter.49.cloned.1.call-update) | async-done | bytes 165904 | tf_op jit(solution)/shard_map/reduce_scatter | solution.py:252
  1209.7 69.6 %reduce-scatter.47.cloned.1.call-done = f32[144,288]{1,0:T(8,128)} async-done(((f32[1152,288]{1,0:T(8,128)}), f32[144,288]{1,0:T(8,128)}) %reduce-scatter.47.cloned.1.call-update) | async-done | bytes 165904 | tf_op jit(solution)/shard_map/reduce_scatter | solution.py:248
  1279.3 69.1 %reduce-scatter.43.cloned.1.call-done = f32[144,288]{1,0:T(8,128)} async-done(((f32[1152,288]{1,0:T(8,128)}), f32[144,288]{1,0:T(8,128)}) %reduce-scatter.43.cloned.1.call-update) | async-done | bytes 165904 | tf_op jit(solution)/shard_map/reduce_scatter | solution.py:246
  1348.4 69.3 %reduce-scatter.45.cloned.1.call-done = f32[144,288]{1,0:T(8,128)} async-done(((f32[1152,288]{1,0:T(8,128)}), f32[144,288]{1,0:T(8,128)}) %reduce-scatter.45.cloned.1.call-update) | async-done | bytes 165904 | tf_op jit(solution)/shard_map/reduce_scatter | solution.py:247
  (572 shorter events, 360.2 us)
Async XLA Ops:
  7.2 135.5 %all-gather.36.cloned.1.call-start = ((), (), s32[]{:S(2)}) async-start(), calls=%async_computation.44 | async-start | bytes 2211840 | tf_op jit(solution)/shard_map/all_gather | solution.py:106
  9.7 152.6 %all-gather.38.cloned.1.call-start = ((), (), s32[]{:S(2)}) async-start(), calls=%async_computation.45 | async-start | bytes 2211840 | tf_op jit(solution)/shard_map/all_gather | solution.py:106
  10.5 171.8 %all-gather.34.cloned.1.call-start = ((), (), s32[]{:S(2)}) async-start(), calls=%async_computation.43 | async-start | bytes 2211840 | tf_op jit(solution)/shard_map/all_gather | solution.py:106
  11.2 193.0 %reduce-scatter.23.cloned.1.call-start = ((), (), s32[]{:S(2)}) async-start(), calls=%async_computation.22 | async-start | bytes 4423680 | tf_op jit(solution)/shard_map/reduce_scatter | solution.py:142
  162.0 85.2 %reduce-scatter.27.cloned.1.call-start = ((), (), s32[]{:S(2)}) async-start(), calls=%async_computation.25 | async-start | bytes 4423680 | tf_op jit(solution)/shard_map/reduce_scatter | solution.py:142
  182.0 108.1 %reduce-scatter.19.cloned.1.call-start = ((), (), s32[]{:S(2)}) async-start(), calls=%async_computation.18 | async-start | bytes 4423680 | tf_op jit(solution)/shard_map/reduce_scatter | solution.py:142
  202.1 161.3 %all-gather.26.cloned.1.call-start = ((), (), s32[]{:S(2)}) async-start(), calls=%async_computation.26 | async-start | bytes 4423680 | tf_op jit(solution)/shard_map/all_gather | solution.py:144
  293.7 78.7 %all-gather.44.cloned.1.call-start = ((), (), s32[]{:S(2)}) async-start(), calls=%async_computation.48 | async-start | bytes 2211840 | tf_op jit(solution)/shard_map/all_gather | solution.py:107
  294.9 110.2 %all-gather.22.cloned.1.call-start = ((), (), s32[]{:S(2)}) async-start(), calls=%async_computation.20 | async-start | bytes 2985984 | tf_op jit(solution)/shard_map/all_gather | solution.py:39
  295.6 140.9 %all-gather.24.cloned.1.call-start = ((), (), s32[]{:S(2)}) async-start(), calls=%async_computation.23 | async-start | bytes 4423680 | tf_op jit(solution)/shard_map/all_gather | solution.py:144
  296.2 162.8 %all-gather.42.cloned.1.call-start = ((), (), s32[]{:S(2)}) async-start(), calls=%async_computation.47 | async-start | bytes 2211840 | tf_op jit(solution)/shard_map/all_gather | solution.py:107
  297.0 194.9 %all-gather.20.cloned.1.call-start = ((), (), s32[]{:S(2)}) async-start(), calls=%async_computation.19 | async-start | bytes 4423680 | tf_op jit(solution)/shard_map/all_gather | solution.py:144
  297.5 217.4 %all-gather.40.cloned.1.call-start = ((), (), s32[]{:S(2)}) async-start(), calls=%async_computation.46 | async-start | bytes 2211840 | tf_op jit(solution)/shard_map/all_gather | solution.py:107
  325.9 16.1 %collective-permute-start.5 = (bf16[144,1076]{1,0:T(8,128)(2,1)S(1)}, bf16[144,1076]{1,0:T(8,128)(2,1)S(1)}, u32[]{:S(2)}, u32[]{:S(2)}) collective-permute-start(bf16[144,1076]{1,0:T(8,128)(2,1)S(1)} %collective-permute-done.4), channel_id=1, source_target_pairs={{0,28},{4,0},{8,4},{12,8},{16,12},{20,16},{24,20},{28,24},{1,29},{... | collective-permute-start | bytes 929672 | tf_op jit(solution)/shard_map/ppermute | solution.py:25
  341.3 216.6 %reduce-scatter.39.cloned.1.call-start = ((), (), s32[]{:S(2)}) async-start(), calls=%async_computation.34 | async-start | bytes 4423680 | tf_op jit(solution)/shard_map/reduce_scatter | solution.py:165
  418.3 182.5 %reduce-scatter.35.cloned.1.call-start = ((), (), s32[]{:S(2)}) async-start(), calls=%async_computation.31 | async-start | bytes 4423680 | tf_op jit(solution)/shard_map/reduce_scatter | solution.py:165
  472.2 171.6 %reduce-scatter.31.cloned.1.call-start = ((), (), s32[]{:S(2)}) async-start(), calls=%async_computation.28 | async-start | bytes 4423680 | tf_op jit(solution)/shard_map/reduce_scatter | solution.py:165
  528.1 161.3 %all-gather.28.cloned.1.call-start = ((), (), s32[]{:S(2)}) async-start(), calls=%async_computation.29 | async-start | bytes 2211840 | tf_op jit(solution)/shard_map/all_gather | solution.py:167
  663.2 61.2 %all-gather.32.cloned.1.call-start = ((), (), s32[]{:S(2)}) async-start(), calls=%async_computation.35 | async-start | bytes 2211840 | tf_op jit(solution)/shard_map/all_gather | solution.py:167
  664.1 95.7 %all-gather.30.cloned.1.call-start = ((), (), s32[]{:S(2)}) async-start(), calls=%async_computation.32 | async-start | bytes 2211840 | tf_op jit(solution)/shard_map/all_gather | solution.py:167
  668.1 179.4 %reduce-scatter.21.cloned.1.call-start = ((), (), s32[]{:S(2)}) async-start(), calls=%async_computation.21 | async-start | bytes 2211840 | tf_op jit(solution)/shard_map/reduce_scatter | solution.py:151
  674.9 172.6 %reduce-scatter.25.cloned.1.call-start = ((), (), s32[]{:S(2)}) async-start(), calls=%async_computation.24 | async-start | bytes 2211840 | tf_op jit(solution)/shard_map/reduce_scatter | solution.py:151
  681.6 165.9 %reduce-scatter.29.cloned.1.call-start = ((), (), s32[]{:S(2)}) async-start(), calls=%async_computation.27 | async-start | bytes 2211840 | tf_op jit(solution)/shard_map/reduce_scatter | solution.py:151
  689.1 173.7 %reduce-scatter.33.cloned.1.call-start = ((), (), s32[]{:S(2)}) async-start(), calls=%async_computation.30 | async-start | bytes 2211840 | tf_op jit(solution)/shard_map/reduce_scatter | solution.py:216
  724.0 166.4 %reduce-scatter.41.cloned.1.call-start = ((), (), s32[]{:S(2)}) async-start(), calls=%async_computation.36 | async-start | bytes 2211840 | tf_op jit(solution)/shard_map/reduce_scatter | solution.py:216
  759.6 163.0 %reduce-scatter.37.cloned.1.call-start = ((), (), s32[]{:S(2)}) async-start(), calls=%async_computation.33 | async-start | bytes 2211840 | tf_op jit(solution)/shard_map/reduce_scatter | solution.py:216
  794.4 236.7 %reduce-scatter.53.cloned.1.call-start = ((), (), s32[]{:S(2)}) async-start(), calls=%async_computation.42 | async-start | bytes 5971968 | tf_op jit(solution)/shard_map/reduce_scatter | solution.py:253
  807.5 332.0 %reduce-scatter.51.cloned.1.call-start = ((), (), s32[]{:S(2)}) async-start(), calls=%async_computation.41 | async-start | bytes 5971968 | tf_op jit(solution)/shard_map/reduce_scatter | solution.py:249
  821.8 387.9 %reduce-scatter.49.cloned.1.call-start = ((), (), s32[]{:S(2)}) async-start(), calls=%async_computation.40 | async-start | bytes 1990656 | tf_op jit(solution)/shard_map/reduce_scatter | solution.py:252
  829.4 449.9 %reduce-scatter.47.cloned.1.call-start = ((), (), s32[]{:S(2)}) async-start(), calls=%async_computation.39 | async-start | bytes 1990656 | tf_op jit(solution)/shard_map/reduce_scatter | solution.py:248
  836.6 511.8 %reduce-scatter.43.cloned.1.call-start = ((), (), s32[]{:S(2)}) async-start(), calls=%async_computation.37 | async-start | bytes 1990656 | tf_op jit(solution)/shard_map/reduce_scatter | solution.py:246
  846.1 571.6 %reduce-scatter.45.cloned.1.call-start = ((), (), s32[]{:S(2)}) async-start(), calls=%async_computation.38 | async-start | bytes 1990656 | tf_op jit(solution)/shard_map/reduce_scatter | solution.py:247
  (171 other events, 2446.5 us)
Sparse Core Ops, SparseCore 0:
  10.2 23.4 all-gather.35
  35.8 20.7 all-gather.37
  58.7 20.7 all-gather.33
  162.2 41.9 reduce-scatter.22
  206.8 40.4 reduce-scatter.26
  249.7 40.4 reduce-scatter.18
  293.9 30.7 all-gather.25
  326.9 20.7 all-gather.43
  350.1 55.0 all-gather.21
  407.2 29.3 all-gather.23
  438.2 20.7 all-gather.41
  461.1 30.7 all-gather.19
  494.1 20.7 all-gather.39
  517.5 40.4 reduce-scatter.38
  560.4 40.4 reduce-scatter.34
  603.4 40.4 reduce-scatter.30
  663.3 21.8 all-gather.27
  687.2 20.7 all-gather.31
  709.6 20.7 all-gather.29
  732.8 29.3 reduce-scatter.20
  765.0 29.3 reduce-scatter.24
  797.0 29.3 reduce-scatter.28
  829.1 29.3 reduce-scatter.32
  861.0 29.3 reduce-scatter.40
  893.1 29.3 reduce-scatter.36
  926.6 104.5 reduce-scatter.52
  1035.6 103.9 reduce-scatter.50
  1143.6 66.1 reduce-scatter.48
  1214.1 65.1 reduce-scatter.46
  1283.2 65.1 reduce-scatter.42
  1352.8 64.7 reduce-scatter.44
